TPU v7x, 512 devices: a whole 4x8x8 slice. The times are simulated.
512 devices in a mesh: row: 8 (over x, core), col: 16 (over y_lo, z), layer: 4 (over y_hi).
Axes of the slice: x: 4, y: 8 (y_hi: 4, y_lo: 2; y = y_hi * 2 + y_lo), z: 8, core: 2. Of those that a mesh axis runs over, the one named last changes fastest.
Arguments:
- hamiltonian: bfloat16 [8192, 8192], P('row', ('col', 'layer')), as said below
- inv_root: bfloat16 [8192, 8192], P('row', 'col'), as said below
- h_pattern: int32 [32, 32], replicated, may hold values from 0 to 1, as said below
- z_pattern: int32 [32, 32], replicated, may hold values from 0 to 1, as said below
Outputs:
- transformed: bfloat16 [8192, 8192], P('row', ('col', 'layer'))
Inputs may be any that keep to these rules, and one draw needn't show every extreme that they name: hamiltonian is symmetric. inv_root is symmetric. h_pattern is symmetric and every diagonal block is present. z_pattern is symmetric and every diagonal block is present.
All inputs are finite; a program needn't handle non-finite values.
Results may differ from a plain program's by a relative error of at most 0.005.
Values may be sent and summed in bfloat16 or wider, within the bound.
A program may use at most 64 MiB of HBM per device.

v0:
```python
import jax
import jax.numpy as jnp
from jax import lax
from jax.sharding import PartitionSpec as P

BS = 256


def mask_tile(tile, pattern, row_start, col_start):
    blocks = pattern.shape[0]
    block_ids = jnp.arange(blocks, dtype=jnp.int32)
    row_ids = (row_start + jnp.arange(tile.shape[0], dtype=jnp.int32)) // BS
    col_ids = (col_start + jnp.arange(tile.shape[1], dtype=jnp.int32)) // BS
    row_pick = (row_ids[:, None] == block_ids[None, :]).astype(jnp.float32)
    col_pick = (block_ids[:, None] == col_ids[None, :]).astype(jnp.float32)
    inner = jnp.dot(pattern.astype(jnp.float32), col_pick, precision=lax.Precision.HIGHEST)
    keep = jnp.dot(row_pick, inner, precision=lax.Precision.HIGHEST)
    return jnp.where(keep > 0.5, tile, jnp.zeros_like(tile))


def accumulate(left, right):
    return jnp.dot(left, right, preferred_element_type=jnp.float32)


def local(hamiltonian, inv_root, h_pattern, z_pattern):
    rows_here = inv_root.shape[0]
    cols_here = inv_root.shape[1]
    quarter = hamiltonian.shape[1]
    layers = lax.axis_size("layer")
    per_row = lax.axis_size("col") // lax.axis_size("row")
    row_index = lax.axis_index("row")
    col_index = lax.axis_index("col")
    layer_index = lax.axis_index("layer")
    h_local = mask_tile(
        hamiltonian, h_pattern, row_index * rows_here, col_index * cols_here + layer_index * quarter
    )
    z_local = mask_tile(inv_root, z_pattern, row_index * rows_here, col_index * cols_here)
    h_whole = lax.all_gather(h_local, "col", axis=1, tiled=True)
    z_layered = z_local.reshape(per_row, layers, quarter, cols_here)
    z_part = lax.dynamic_index_in_dim(z_layered, layer_index, 1, keepdims=False).reshape(
        per_row * quarter, cols_here
    )
    columns = h_whole
    partial_y = accumulate(columns, lax.all_gather(z_part, "row", axis=0, tiled=True))
    z_quarter = lax.dynamic_slice_in_dim(z_local, layer_index * quarter, quarter, 1)
    z_rows = lax.all_gather(z_quarter, "col", axis=1, tiled=True)
    summed = lax.psum(partial_y, "layer")
    layered = summed.reshape(per_row, layers, quarter, cols_here)
    own_rows = lax.dynamic_index_in_dim(layered, layer_index, 1, keepdims=False).reshape(
        per_row * quarter, cols_here
    )
    y_own = own_rows.astype(jnp.bfloat16)
    columns = z_rows
    partial_c = accumulate(columns, lax.all_gather(y_own, "row", axis=0, tiled=True))
    result = lax.psum_scatter(partial_c, "layer", scatter_dimension=1, tiled=True)
    return result.astype(jnp.bfloat16)


def solution(mesh):
    return jax.shard_map(
        local,
        mesh=mesh,
        in_specs=(P("row", ("col", "layer")), P("row", "col"), P(), P()),
        out_specs=P("row", ("col", "layer")),
        check_vma=False,
    )
```

profile of v0, /device:TPU:20, one launch (start us, length us, event | category | flops | bytes accessed | tf_op | source)
XLA Modules:
  0.0 365.5 jit_solution(18108361089963021768)
XLA Ops:
  6.5 0.0 copy-start
  6.5 0.0 copy-start.1
  6.5 0.0 all-gather.9.cloned.1.call-start
  6.6 1.1 fusion.4
  7.7 2.3 compare_select_fusion
  10.0 0.7 constant_dynamic-slice_fusion
  10.7 0.0 all-gather.9.cloned.1.call-update
  10.7 0.0 all-gather.7.cloned.1.call-start
  10.8 0.0 copy-done
  10.8 0.2 fusion.7
  11.1 0.0 copy-done.1
  11.1 1.2 fusion
  12.2 0.0 all-gather.7.cloned.1.call-update
  12.3 0.0 all-gather.5.cloned.1.call-start
  12.3 0.7 constant_dynamic-slice_fusion.1
  13.1 0.0 all-gather.5.cloned.1.call-update
  13.1 0.0 all-gather.11.cloned.1.call-start
  13.1 31.7 %all-gather.9.cloned.1.call-done = bf16[2048,512]{1,0:T(8,128)(2,1)} async-done(((bf16[256,512]{1,0:T(8,128)(2,1)}), bf16[2048,512]{1,0:T(8,128)(2,1)}) %all-gather.9.cloned.1.call-update) | async-done | bytes 2097168 | tf_op jit(solution)/shard_map/all_gather | solution.py:44
  44.9 95.0 %all-gather.7.cloned.1.call-done = bf16[1024,2048]{1,0:T(8,128)(2,1)} async-done(((bf16[1024,128]{1,0:T(8,128)(2,1)}), bf16[1024,2048]{1,0:T(8,128)(2,1)}) %all-gather.7.cloned.1.call-update) | async-done | bytes 4194320 | tf_op jit(solution)/shard_map/all_gather | solution.py:38
  139.8 5.2 %fusion.19 = f32[1024,512]{1,0:T(8,128)S(1)} fusion(bf16[1024,2048]{1,0:T(8,128)(2,1)} %all-gather.7.cloned.1.call-done, bf16[2048,512]{1,0:T(8,128)(2,1)} %all-gather.9.cloned.1.call-done), kind=kOutput, calls=%fused_computation.41 | convolution fusion | flops 2147483648 | bytes 8388608 | tf_op jit(solution)/shard_map/dot_general | solution.py:22
  145.0 90.8 %all-reduce.1 = bf16[2,4,128,512]{3,2,1,0:T(8,128)(2,1)S(1)} all-reduce(f32[2,4,128,512]{3,2,1,0:T(8,128)S(1)} %bitcast.10), channel_id=1, replica_groups=mesh['row'=8,'col'=16,'layer'=4] {'layer'}, use_global_device_ids=true, to_apply=%region_0.1 | all-reduce | flops 524288 | bytes 3145728 | tf_op jit(solution)/shard_map/psum | solution.py:47
  235.8 0.7 dynamic-slice_convert_fusion
  236.6 0.0 all-gather.11.cloned.1.call-update
  236.6 0.0 reduce-scatter.2.cloned.1.call-start
  236.6 30.9 %all-gather.5.cloned.1.call-done = bf16[1024,2048]{1,0:T(8,128)(2,1)} async-done(((bf16[1024,128]{1,0:T(8,128)(2,1)}), bf16[1024,2048]{1,0:T(8,128)(2,1)}) %all-gather.5.cloned.1.call-update) | async-done | bytes 4194320 | tf_op jit(solution)/shard_map/all_gather | solution.py:46
  267.5 28.2 %all-gather.11.cloned.1.call-done = bf16[2048,512]{1,0:T(8,128)(2,1)} async-done(((bf16[256,512]{1,0:T(8,128)(2,1)}), bf16[2048,512]{1,0:T(8,128)(2,1)}) %all-gather.11.cloned.1.call-update) | async-done | bytes 2097168 | tf_op jit(solution)/shard_map/all_gather | solution.py:54
  295.6 6.5 %fusion.20 = f32[1024,512]{1,0:T(8,128)} fusion(bf16[1024,2048]{1,0:T(8,128)(2,1)} %all-gather.5.cloned.1.call-done, bf16[2048,512]{1,0:T(8,128)(2,1)} %all-gather.11.cloned.1.call-done), kind=kOutput, calls=%fused_computation.42 | convolution fusion | flops 2147483648 | bytes 8388608 | tf_op jit(solution)/shard_map/dot_general | solution.py:22
  302.2 0.0 reduce-scatter.2.cloned.1.call-update
  302.2 55.0 %reduce-scatter.2.cloned.1.call-done = f32[1024,128]{1,0:T(8,128)} async-done(((f32[1024,512]{1,0:T(8,128)}), f32[1024,128]{1,0:T(8,128)}) %reduce-scatter.2.cloned.1.call-update) | async-done | bytes 524304 | tf_op jit(solution)/shard_map/reduce_scatter | solution.py:55
  357.2 1.8 convert_element_type.23
  (3 shorter events, 0.0 us)
Async XLA Ops:
  6.5 4.3 %copy-start = (s32[32,32]{1,0:T(8,128)S(1)}, s32[32,32]{1,0:T(8,128)}, u32[]{:S(2)}) copy-start(s32[32,32]{1,0:T(8,128)} %param.6) | copy-start | bytes 12292
  6.5 4.5 %copy-start.1 = (bf16[1024,128]{1,0:T(8,128)(2,1)S(1)}, bf16[1024,128]{1,0:T(8,128)(2,1)}, u32[]{:S(2)}) copy-start(bf16[1024,128]{1,0:T(8,128)(2,1)} %param.4) | copy-start | bytes 786436
  6.5 38.3 %all-gather.9.cloned.1.call-start = ((), (), s32[]{:S(2)}) async-start(), calls=%async_computation.3 | async-start | bytes 2359296 | tf_op jit(solution)/shard_map/all_gather | solution.py:44
  10.7 129.1 %all-gather.7.cloned.1.call-start = ((), (), s32[]{:S(2)}) async-start(), calls=%async_computation.2 | async-start | bytes 4456448 | tf_op jit(solution)/shard_map/all_gather | solution.py:38
  12.3 255.2 %all-gather.5.cloned.1.call-start = ((), (), s32[]{:S(2)}) async-start(), calls=%async_computation.1 | async-start | bytes 4456448 | tf_op jit(solution)/shard_map/all_gather | solution.py:46
  13.1 282.6 %all-gather.11.cloned.1.call-start = ((), (), s32[]{:S(2)}) async-start(), calls=%async_computation.4 | async-start | bytes 2359296 | tf_op jit(solution)/shard_map/all_gather | solution.py:54
  236.6 120.7 %reduce-scatter.2.cloned.1.call-start = ((), (), s32[]{:S(2)}) async-start(), calls=%async_computation.5 | async-start | bytes 2621440 | tf_op jit(solution)/shard_map/reduce_scatter | solution.py:55
Sparse Core Ops, SparseCore 0:
  10.9 33.9 all-gather.8
  46.9 92.9 all-gather.6
  141.9 125.5 all-gather.4
  269.5 26.1 all-gather.10
  302.3 54.8 reduce-scatter.1
where the time goes:
time: 366 us
  waiting for transfers between devices  241 us (66%)
  blocking collectives  90.8 us (25%)
  matrix products  16.5 us (5%)
  between operations  13.2 us (4%)
    all_gather x1, waiting for transfers between devices, local(): h_whole = lax.all_gather(h_local, 'col', axis=1, tiled=True)  95 us
    psum x1, blocking collectives, local(): summed = lax.psum(partial_y, 'layer')  90.8 us
    reduce_scatter x1, waiting for transfers between devices, local(): lax.psum_scatter(partial_c, 'layer', scatter_dimension=1, tiled=True)  55 us
    all_gather x1, waiting for transfers between devices, local(): lax.all_gather(z_part, 'row', axis=0, tiled=True)  31.7 us
    all_gather x1, waiting for transfers between devices, local(): z_rows = lax.all_gather(z_quarter, 'col', axis=1, tiled=True)  30.9 us
    all_gather x1, waiting for transfers between devices, local(): lax.all_gather(y_own, 'row', axis=0, tiled=True)  28.2 us
    dot_general x2, matrix products, accumulate(): return jnp.dot(left, right, preferred_element_type=jnp.float32)  11.7 us
  transfers between devices with their start and end apart: 5, of which 5 were waited for; matrix products, arithmetic and copies ran while one was open for 2% of the time, Pallas kernels for 0%

commit v1 on v0

--- a/solution.py
+++ b/solution.py
@@ -41,7 +41,12 @@
         per_row * quarter, cols_here
     )
     columns = h_whole
-    partial_y = accumulate(columns, lax.all_gather(z_part, "row", axis=0, tiled=True))
+    partial_y = accumulate(
+        columns,
+        jnp.concatenate(
+            lax.all_to_all(jnp.stack([z_part] * lax.axis_size("row")), "row", 0, 0), axis=0
+        ),
+    )
     z_quarter = lax.dynamic_slice_in_dim(z_local, layer_index * quarter, quarter, 1)
     z_rows = lax.all_gather(z_quarter, "col", axis=1, tiled=True)
     summed = lax.psum(partial_y, "layer")

time: 366 us -> 332 us (0.907)
  waiting for transfers between devices: 241 us -> 176 us
  blocking collectives: 90.8 us -> 120 us
    all_gather x1, waiting for transfers between devices: 95 us -> 62.3 us  [local(): h_whole = lax.all_gather(h_local, 'col', axis=1, tiled=True)]
    all_gather x1 -> x0, waiting for transfers between devices: 31.7 us -> none  [local(): lax.all_gather(z_part, 'row', axis=0, tiled=True)]
    all_to_all x0 -> x1, blocking collectives: none -> 29 us  [local(): lax.all_to_all(jnp.stack([z_part] * lax.axis_size('row')), 'row', 0, 0)]
  transfers between devices with their start and end apart: 5 -> 4, of which waited for: 5 -> 4; matrix products, arithmetic and copies ran while one was open for 2% -> 3% of each run, Pallas kernels for 0% -> 0%
where the time goes in v1:
time: 332 us; the launch traced here: 331 us
  waiting for transfers between devices  176 us (53%)
  blocking collectives  120 us (36%)
  matrix products  18.1 us (5%)
  between operations  13.2 us (4%)
    psum x1, blocking collectives, local(): summed = lax.psum(partial_y, 'layer')  91.1 us
    all_gather x1, waiting for transfers between devices, local(): h_whole = lax.all_gather(h_local, 'col', axis=1, tiled=True)  62.3 us
    reduce_scatter x1, waiting for transfers between devices, local(): lax.psum_scatter(partial_c, 'layer', scatter_dimension=1, tiled=True)  55 us
    all_gather x1, waiting for transfers between devices, local(): z_rows = lax.all_gather(z_quarter, 'col', axis=1, tiled=True)  32.6 us
    all_to_all x1, blocking collectives, local(): lax.all_to_all(jnp.stack([z_part] * lax.axis_size('row')), 'row', 0, 0)  29 us
    all_gather x1, waiting for transfers between devices, local(): lax.all_gather(y_own, 'row', axis=0, tiled=True)  26.2 us
    dot_general x2, matrix products, accumulate(): return jnp.dot(left, right, preferred_element_type=jnp.float32)  11.7 us
  transfers between devices with their start and end apart: 4, of which 4 were waited for; matrix products, arithmetic and copies ran while one was open for 3% of the time, Pallas kernels for 0%

profile of v1, /device:TPU:20, one launch (start us, length us, event | category | flops | bytes accessed | tf_op | source)
XLA Modules:
  0.0 331.3 jit_solution(8961672739624774602)
XLA Ops:
  6.5 0.0 all-gather.6.cloned.1.call-start
  6.6 1.0 fusion.7
  7.5 2.1 fusion
  9.7 0.0 all-gather.6.cloned.1.call-update
  9.7 0.0 all-gather.4.cloned.1.call-start
  9.7 1.0 fusion.4
  10.8 2.3 compare_select_fusion
  13.1 0.7 constant_dynamic-slice_fusion.1
  13.9 0.0 all-gather.4.cloned.1.call-update
  13.9 0.0 all-gather.8.cloned.1.call-start
  14.0 0.2 stack.3
  14.1 29.0 %all_to_all.5 = bf16[8,256,512]{2,1,0:T(8,128)(2,1)} all-to-all(bf16[8,256,512]{2,1,0:T(8,128)(2,1)S(1)} %stack.3), channel_id=1, replica_groups=mesh['row'=8,'col'=16,'layer'=4] {'row'}, dimensions={0} | all-to-all | bytes 4194304 | tf_op jit(solution)/shard_map/all_to_all | solution.py:47
  43.2 62.3 %all-gather.6.cloned.1.call-done = bf16[1024,2048]{1,0:T(8,128)(2,1)} async-done(((bf16[1024,128]{1,0:T(8,128)(2,1)}), bf16[1024,2048]{1,0:T(8,128)(2,1)}) %all-gather.6.cloned.1.call-update) | async-done | bytes 4194320 | tf_op jit(solution)/shard_map/all_gather | solution.py:38
  105.5 5.2 %fusion.19 = f32[1024,512]{1,0:T(8,128)S(1)} fusion(bf16[1024,2048]{1,0:T(8,128)(2,1)} %all-gather.6.cloned.1.call-done, bf16[2048,512]{1,0:T(8,128)(2,1)} %bitcast.12), kind=kOutput, calls=%fused_computation.41 | convolution fusion | flops 2147483648 | bytes 8388608 | tf_op jit(solution)/shard_map/dot_general | solution.py:22
  110.7 91.1 %all-reduce.1 = bf16[2,4,128,512]{3,2,1,0:T(8,128)(2,1)S(1)} all-reduce(f32[2,4,128,512]{3,2,1,0:T(8,128)S(1)} %bitcast.11), channel_id=1, replica_groups=mesh['row'=8,'col'=16,'layer'=4] {'layer'}, use_global_device_ids=true, to_apply=%region_0.1 | all-reduce | flops 524288 | bytes 3145728 | tf_op jit(solution)/shard_map/psum | solution.py:52
  201.8 0.7 dynamic-slice_convert_fusion
  202.5 0.0 all-gather.8.cloned.1.call-update
  202.6 0.0 reduce-scatter.2.cloned.1.call-start
  202.6 32.6 %all-gather.4.cloned.1.call-done = bf16[1024,2048]{1,0:T(8,128)(2,1)} async-done(((bf16[1024,128]{1,0:T(8,128)(2,1)}), bf16[1024,2048]{1,0:T(8,128)(2,1)}) %all-gather.4.cloned.1.call-update) | async-done | bytes 4194320 | tf_op jit(solution)/shard_map/all_gather | solution.py:51
  235.2 26.2 %all-gather.8.cloned.1.call-done = bf16[2048,512]{1,0:T(8,128)(2,1)} async-done(((bf16[256,512]{1,0:T(8,128)(2,1)}), bf16[2048,512]{1,0:T(8,128)(2,1)}) %all-gather.8.cloned.1.call-update) | async-done | bytes 2097168 | tf_op jit(solution)/shard_map/all_gather | solution.py:59
  261.4 6.5 %fusion.20 = f32[1024,512]{1,0:T(8,128)} fusion(bf16[1024,2048]{1,0:T(8,128)(2,1)} %all-gather.4.cloned.1.call-done, bf16[2048,512]{1,0:T(8,128)(2,1)} %all-gather.8.cloned.1.call-done), kind=kOutput, calls=%fused_computation.42 | convolution fusion | flops 2147483648 | bytes 8388608 | tf_op jit(solution)/shard_map/dot_general | solution.py:22
  267.9 0.0 reduce-scatter.2.cloned.1.call-update
  268.0 55.0 %reduce-scatter.2.cloned.1.call-done = f32[1024,128]{1,0:T(8,128)} async-done(((f32[1024,512]{1,0:T(8,128)}), f32[1024,128]{1,0:T(8,128)}) %reduce-scatter.2.cloned.1.call-update) | async-done | bytes 524304 | tf_op jit(solution)/shard_map/reduce_scatter | solution.py:60
  323.0 1.8 convert_element_type.23
  (4 shorter events, 0.1 us)
Async XLA Ops:
  6.5 98.9 %all-gather.6.cloned.1.call-start = ((), (), s32[]{:S(2)}) async-start(), calls=%async_computation.3 | async-start | bytes 4456448 | tf_op jit(solution)/shard_map/all_gather | solution.py:38
  9.7 225.5 %all-gather.4.cloned.1.call-start = ((), (), s32[]{:S(2)}) async-start(), calls=%async_computation.2 | async-start | bytes 4456448 | tf_op jit(solution)/shard_map/all_gather | solution.py:51
  13.9 247.5 %all-gather.8.cloned.1.call-start = ((), (), s32[]{:S(2)}) async-start(), calls=%async_computation.4 | async-start | bytes 2359296 | tf_op jit(solution)/shard_map/all_gather | solution.py:59
  202.6 120.5 %reduce-scatter.2.cloned.1.call-start = ((), (), s32[]{:S(2)}) async-start(), calls=%async_computation.5 | async-start | bytes 2621440 | tf_op jit(solution)/shard_map/reduce_scatter | solution.py:60
Sparse Core Ops, SparseCore 0:
  9.8 95.6 all-gather.5
  107.5 127.6 all-gather.3
  237.3 24.0 all-gather.7
  268.1 54.8 reduce-scatter.1

commit v2 on v0

--- a/solution.py
+++ b/solution.py
@@ -44,7 +44,7 @@
     partial_y = accumulate(columns, lax.all_gather(z_part, "row", axis=0, tiled=True))
     z_quarter = lax.dynamic_slice_in_dim(z_local, layer_index * quarter, quarter, 1)
     z_rows = lax.all_gather(z_quarter, "col", axis=1, tiled=True)
-    summed = lax.psum(partial_y, "layer")
+    summed = jnp.sum(lax.all_gather(partial_y, "layer"), axis=0)
     layered = summed.reshape(per_row, layers, quarter, cols_here)
     own_rows = lax.dynamic_index_in_dim(layered, layer_index, 1, keepdims=False).reshape(
         per_row * quarter, cols_here

time: 366 us -> 497 us (1.36)
  the two profiles are of different devices: /device:TPU:20 before, /device:TPU:22 now
where the time goes in v2:
time: 497 us
  waiting for transfers between devices  457 us (92%)
  matrix products  17.8 us (4%)
  between operations  13.5 us (3%)
  other arithmetic  6.37 us (1%)
    all_gather x1, waiting for transfers between devices, local(): summed = jnp.sum(lax.all_gather(partial_y, 'layer'), axis=0)  153 us
    all_gather x1, waiting for transfers between devices, local(): h_whole = lax.all_gather(h_local, 'col', axis=1, tiled=True)  95 us
    all_gather x1, waiting for transfers between devices, local(): z_rows = lax.all_gather(z_quarter, 'col', axis=1, tiled=True)  91.5 us
    reduce_scatter x1, waiting for transfers between devices, local(): lax.psum_scatter(partial_c, 'layer', scatter_dimension=1, tiled=True)  55 us
    all_gather x1, waiting for transfers between devices, local(): lax.all_gather(z_part, 'row', axis=0, tiled=True)  32.5 us
    all_gather x1, waiting for transfers between devices, local(): lax.all_gather(y_own, 'row', axis=0, tiled=True)  30.4 us
    dot_general x2, matrix products, accumulate(): return jnp.dot(left, right, preferred_element_type=jnp.float32)  13 us
  transfers between devices with their start and end apart: 6, of which 6 were waited for; matrix products, arithmetic and copies ran while one was open for 2% of the time, Pallas kernels for 0%

profile of v2, /device:TPU:22, one launch (start us, length us, event | category | flops | bytes accessed | tf_op | source)
XLA Modules:
  0.0 497.2 jit_solution(2216060005166319755)
XLA Ops:
  6.5 0.0 copy-start
  6.5 0.0 copy-start.1
  6.5 0.0 all-gather.11.cloned.1.call-start
  6.6 1.1 fusion.4
  7.7 2.3 compare_select_fusion
  10.0 0.7 constant_dynamic-slice_fusion
  10.7 0.0 all-gather.11.cloned.1.call-update
  10.7 0.0 all-gather.9.cloned.1.call-start
  10.8 0.0 copy-done
  10.8 0.2 fusion.7
  11.0 0.0 copy-done.1
  11.1 1.2 fusion
  12.2 0.0 all-gather.9.cloned.1.call-update
  12.2 0.0 all-gather.15.cloned.1.call-start
  12.3 32.5 %all-gather.11.cloned.1.call-done = bf16[2048,512]{1,0:T(8,128)(2,1)} async-done(((bf16[256,512]{1,0:T(8,128)(2,1)}), bf16[2048,512]{1,0:T(8,128)(2,1)}) %all-gather.11.cloned.1.call-update) | async-done | bytes 2097168 | tf_op jit(solution)/shard_map/all_gather | solution.py:44
  44.8 95.0 %all-gather.9.cloned.1.call-done = bf16[1024,2048]{1,0:T(8,128)(2,1)} async-done(((bf16[1024,128]{1,0:T(8,128)(2,1)}), bf16[1024,2048]{1,0:T(8,128)(2,1)}) %all-gather.9.cloned.1.call-update) | async-done | bytes 4194320 | tf_op jit(solution)/shard_map/all_gather | solution.py:38
  139.8 6.5 %fusion.19 = f32[1024,512]{1,0:T(8,128)} fusion(bf16[1024,2048]{1,0:T(8,128)(2,1)} %all-gather.9.cloned.1.call-done, bf16[2048,512]{1,0:T(8,128)(2,1)} %all-gather.11.cloned.1.call-done), kind=kOutput, calls=%fused_computation.41 | convolution fusion | flops 2147483648 | bytes 8388608 | tf_op jit(solution)/shard_map/dot_general | solution.py:22
  146.3 0.0 all-gather.15.cloned.1.call-update
  146.3 0.0 all-gather.7.cloned.1.call-start
  146.4 0.7 constant_dynamic-slice_fusion.1
  147.1 0.0 all-gather.7.cloned.1.call-update
  147.2 0.0 all-gather.13.cloned.1.call-start
  147.2 152.5 %all-gather.15.cloned.1.call-done = f32[4096,512]{1,0:T(8,128)} async-done(((f32[1024,512]{1,0:T(8,128)}), f32[4096,512]{1,0:T(8,128)}) %all-gather.15.cloned.1.call-update) | async-done | bytes 8388624 | tf_op jit(solution)/shard_map/all_gather | solution.py:47
  299.7 4.6 reduce_sum.9
  304.3 0.7 dynamic-slice_convert_fusion
  305.1 0.0 all-gather.13.cloned.1.call-update
  305.1 0.0 reduce-scatter.2.cloned.1.call-start
  305.1 91.5 %all-gather.7.cloned.1.call-done = bf16[1024,2048]{1,0:T(8,128)(2,1)} async-done(((bf16[1024,128]{1,0:T(8,128)(2,1)}), bf16[1024,2048]{1,0:T(8,128)(2,1)}) %all-gather.7.cloned.1.call-update) | async-done | bytes 4194320 | tf_op jit(solution)/shard_map/all_gather | solution.py:46
  396.6 30.4 %all-gather.13.cloned.1.call-done = bf16[2048,512]{1,0:T(8,128)(2,1)} async-done(((bf16[256,512]{1,0:T(8,128)(2,1)}), bf16[2048,512]{1,0:T(8,128)(2,1)}) %all-gather.13.cloned.1.call-update) | async-done | bytes 2097168 | tf_op jit(solution)/shard_map/all_gather | solution.py:54
  427.0 6.5 %fusion.20 = f32[1024,512]{1,0:T(8,128)} fusion(bf16[1024,2048]{1,0:T(8,128)(2,1)} %all-gather.7.cloned.1.call-done, bf16[2048,512]{1,0:T(8,128)(2,1)} %all-gather.13.cloned.1.call-done), kind=kOutput, calls=%fused_computation.42 | convolution fusion | flops 2147483648 | bytes 8388608 | tf_op jit(solution)/shard_map/dot_general | solution.py:22
  433.5 0.0 reduce-scatter.2.cloned.1.call-update
  433.6 55.0 %reduce-scatter.2.cloned.1.call-done = f32[1024,128]{1,0:T(8,128)} async-done(((f32[1024,512]{1,0:T(8,128)}), f32[1024,128]{1,0:T(8,128)}) %reduce-scatter.2.cloned.1.call-update) | async-done | bytes 524304 | tf_op jit(solution)/shard_map/reduce_scatter | solution.py:55
  488.6 1.8 convert_element_type.23
  (3 shorter events, 0.0 us)
Async XLA Ops:
  6.5 4.3 copy-start
  6.5 4.5 copy-start.1
  6.5 38.3 %all-gather.11.cloned.1.call-start = ((), (), s32[]{:S(2)}) async-start(), calls=%async_computation.3 | async-start | bytes 2359296 | tf_op jit(solution)/shard_map/all_gather | solution.py:44
  10.7 129.1 %all-gather.9.cloned.1.call-start = ((), (), s32[]{:S(2)}) async-start(), calls=%async_computation.2 | async-start | bytes 4456448 | tf_op jit(solution)/shard_map/all_gather | solution.py:38
  12.2 287.5 %all-gather.15.cloned.1.call-start = ((), (), s32[]{:S(2)}) async-start(), calls=%async_computation.6 | async-start | bytes 10485760 | tf_op jit(solution)/shard_map/all_gather | solution.py:47
  146.3 250.3 %all-gather.7.cloned.1.call-start = ((), (), s32[]{:S(2)}) async-start(), calls=%async_computation.1 | async-start | bytes 4456448 | tf_op jit(solution)/shard_map/all_gather | solution.py:46
  147.2 279.9 %all-gather.13.cloned.1.call-start = ((), (), s32[]{:S(2)}) async-start(), calls=%async_computation.4 | async-start | bytes 2359296 | tf_op jit(solution)/shard_map/all_gather | solution.py:54
  305.1 183.5 %reduce-scatter.2.cloned.1.call-start = ((), (), s32[]{:S(2)}) async-start(), calls=%async_computation.5 | async-start | bytes 2621440 | tf_op jit(solution)/shard_map/reduce_scatter | solution.py:55
Sparse Core Ops, SparseCore 0:
  10.8 33.9 all-gather.10
  46.8 92.9 all-gather.8
  146.5 153.2 all-gather.14
  301.6 94.9 all-gather.6
  398.6 28.3 all-gather.12
  433.7 54.8 reduce-scatter.1
